TPU v7x, 32 devices: a whole 2x2x4 slice. The times are simulated.
32 devices in a mesh: grp: 2 (over y), tm: 4 (over z), sub: 2 (over x), ch: 2 (over core).
Axes of the slice: x: 2, y: 2, z: 4, core: 2. Of those that a mesh axis runs over, the one named last changes fastest.
Arguments:
- archive: float32 [16, 16384], P('ch', ('grp', 'tm')), parts along dimension 1, may hold values from -6 to 6
- tail: float32 [16, 254], P(None, 'grp'), parts along dimension 1, may hold values from -6 to 6
- precision: float32 [16, 16], replicated, may hold values from -1.5 to 1.5
- tile_list: int32 [8, 2, 2, 2], P(('grp', 'tm'), 'sub'), parts along dimension 0, may hold values from 0 to 15, as said below
Outputs:
- profile: float32 [16384], P(('grp', 'tm', 'sub')), parts along dimension 0
There are 2 independent parts, one for each index of `grp`. A program takes and returns all parts, laid end to end along the dimension named above; an argument that names none is the same for every part. Nothing has to cross between parts.
Inputs may be any that keep to these rules, and one draw needn't show every extreme that they name: `tile_list`: each pair has row block <= column block; every block k < 16 appears in some pair; pairs may repeat.
All inputs are finite; a program needn't handle non-finite values.
Results may differ from a plain program's by a relative error of at most 0.0003.
Values may be sent and summed in bfloat16 or wider, within the bound.
A program may use at most 128 MiB of HBM per device.

v0:
```python
import functools

import jax
import jax.numpy as jnp
from jax import lax
from jax.experimental import pallas as pl
from jax.experimental.pallas import tpu as pltpu
from jax.sharding import PartitionSpec as P

M = 128
TS = 512
SLOTS = 2
DEPTH = 2048
EXCL = 32
LANES = 128
STEP = 16
JOIN = 2
PAIRED = 2
MESH = pl.DeviceIdType.MESH


def whiten(factor, samples):
    return jnp.dot(
        factor, samples, precision=lax.Precision.HIGHEST, preferred_element_type=jnp.float32
    ).astype(jnp.bfloat16)


def lag(series_ref, first_tile, count, scale):
    channels = series_ref.shape[1]
    pieces = [series_ref[first_tile + k].astype(jnp.float32) for k in range(count)]
    segment = jnp.concatenate(pieces, axis=1)
    width = count * LANES
    column = lax.broadcasted_iota(jnp.int32, (channels, LANES), 1)
    turned = {}

    def turn(k, l):
        k = min(k, count - 1)
        if (k, l) not in turned:
            turned[k, l] = pieces[k] if l == 0 else pltpu.roll(pieces[k], LANES - l, axis=1)
        return turned[k, l]

    def moved(k, l):
        here = turn(k, l)
        here = here if l == 0 else jnp.where(column < LANES - l, here, turn(k + 1, l))
        return here.astype(jnp.bfloat16)

    near = []
    for at in range(0, count, 2):
        tiles = range(at, min(at + 2, count))
        hankel = jnp.concatenate(
            [jnp.concatenate([moved(k, l) for k in tiles], axis=1) for l in range(8)], axis=0
        )
        size = len(tiles) * LANES
        unit_matrix = jnp.where(
            lax.broadcasted_iota(jnp.int32, (size, size), 0)
            == lax.broadcasted_iota(jnp.int32, (size, size), 1),
            scale,
            0.0,
        ).astype(jnp.bfloat16)
        near.append(
            lax.dot_general(
                unit_matrix, hankel, (((1,), (1,)), ((), ())), preferred_element_type=jnp.float32
            )
        )
    lagged = []
    for at, piece in enumerate(near):
        after = near[min(at + 1, len(near) - 1)]
        late = jnp.concatenate([piece[8:], after[:8]], axis=0)
        lagged.append(
            jnp.concatenate([piece.astype(jnp.bfloat16), late.astype(jnp.bfloat16)], axis=1)
        )
    norms = jnp.broadcast_to(jnp.sum(segment * segment, axis=0, keepdims=True), (8, width))
    shift = 1
    while shift < M:
        norms = norms + pltpu.roll(norms, width - shift, axis=1)
        shift *= 2
    return lagged, norms


def own_columns(series_ref, own_tile, mine_ref, norms_ref):
    units, unit_cols, joined = mine_ref.shape
    depth = joined // JOIN
    n_tiles = unit_cols // LANES
    unit = unit_cols - M
    lagged, norms_ref[...] = lag(series_ref, own_tile, units * unit // LANES + 1, 1.0)
    groups = [piece[at : at + STEP] for piece in lagged for at in range(0, piece.shape[0], STEP)]
    for u in range(units):
        for q in range(unit_cols // STEP):
            place = ((q % n_tiles) * 8 + q // n_tiles) * STEP
            for v in range(JOIN):
                at = min(u * unit // STEP + q + v, len(groups) - 1)
                mine_ref[u, place : place + STEP, v * depth : (v + 1) * depth] = groups[at]


def gather_kernel(
    n_tm,
    n_sub,
    tiles_hbm,
    archive_hbm,
    tail_hbm,
    precision_hbm,
    series_ref,
    lists_smem,
    mine_ref,
    norms_ref,
    lists_ref,
    tail_ref,
    precision_ref,
    raw_ref,
    load_sems,
    raw_sems,
    time_send,
    time_recv,
    pair_send,
    pair_recv,
    list_send,
    list_recv,
    here_sems,
):
    tm, sub, ch = lax.axis_index("tm"), lax.axis_index("sub"), lax.axis_index("ch")
    other = 1 - ch
    owners = n_tm * n_sub
    me = tm * n_sub + sub
    channels, span = archive_hbm.shape
    half = span // 2
    tiles = half // LANES
    last = n_tm * span // LANES

    def send(source, target, sem, landed, device):
        return pltpu.make_async_remote_copy(
            src_ref=source,
            dst_ref=target,
            send_sem=sem,
            recv_sem=landed,
            device_id=device,
            device_id_type=MESH,
        )

    def each_owner(action):
        if owners <= 16:
            for rank in range(owners):
                action(rank, rank // n_sub, rank % n_sub)
        else:
            lax.fori_loop(
                0, owners, lambda rank, _: (action(rank, rank // n_sub, rank % n_sub), 0)[1], 0
            )

    def above(rank, t, s):
        return (t >= tm) & (s >= sub) & (rank != me)

    def below(rank, t, s):
        return (t <= tm) & (s <= sub) & (rank != me)

    barrier = pltpu.get_barrier_semaphore()
    pl.semaphore_signal(barrier, inc=1, device_id={"ch": other}, device_id_type=MESH)

    def announce(rank, t, s):
        @pl.when(above(rank, t, s))
        def _():
            pl.semaphore_signal(
                barrier, inc=1, device_id={"tm": t, "sub": s}, device_id_type=MESH
            )

    own_rows = pl.ds(pl.multiple_of(ch * channels, channels), channels)
    own_half = archive_hbm.at[:, pl.ds(pl.multiple_of(ch * half, half), half)]
    own_list = lists_ref.at[me]
    loads = [
        pltpu.make_async_copy(source, target, load_sems.at[at])
        for at, (source, target) in enumerate(
            (
                (precision_hbm, precision_ref),
                (tail_hbm, tail_ref),
                (own_half, raw_ref.at[own_rows, :]),
                (tiles_hbm.at[0, 0], own_list),
            )
        )
    ]
    for load in loads:
        load.start()
    each_owner(announce)
    pl.semaphore_wait(barrier, (tm + 1) * (sub + 1))

    swap = send(
        archive_hbm.at[:, pl.ds(pl.multiple_of(other * half, half), half)],
        raw_ref.at[own_rows, :],
        raw_sems.at[0],
        raw_sems.at[1],
        {"ch": other},
    )
    swap.start()

    def direct(rank, t, s):
        return send(
            tiles_hbm.at[0, 0],
            own_list,
            list_send.at[rank],
            list_recv.at[me],
            {"tm": t, "sub": s},
        )

    def answer(rank, t, s):
        @pl.when(below(rank, t, s))
        def _():
            pl.semaphore_signal(
                here_sems.at[me], inc=1, device_id={"tm": t, "sub": s}, device_id_type=MESH
            )
            direct(rank, t, s).start()

    each_owner(answer)
    for load in loads[:2]:
        load.wait()
    factor = precision_ref[...]
    series_ref[last] = jnp.zeros((2 * channels, LANES), jnp.bfloat16)
    series_ref[last, :, : M - 1] = whiten(factor, tail_ref[...])
    for load in loads[2:]:
        load.wait()
    swap.wait_recv()

    def chunk(owner, part):
        return series_ref.at[pl.ds((owner * 2 + part) * tiles, tiles)]

    mine = chunk(tm, ch)
    whitened = whiten(factor, raw_ref[...])
    for k in range(tiles):
        series_ref[(tm * 2 + ch) * tiles + k] = whitened[:, k * LANES : (k + 1) * LANES]

    def along_time(t):
        return send(mine, mine, time_send.at[t], time_recv.at[tm], {"tm": t})

    to_pair = []

    def forward(held):
        step = len(to_pair)
        copy = send(held, held, pair_send.at[step], pair_recv.at[step], {"ch": other})
        to_pair.append(copy)
        copy.start()

    for t in range(n_tm):
        pl.when(t < tm)(along_time(t).start)
    forward(mine)
    for t in range(1, n_tm):

        @pl.when(t > tm)
        def _():
            pl.semaphore_wait(here_sems.at[t * n_sub + sub], 1)
            along_time(t).start()
            for s in range(n_sub):
                pl.when(s <= sub)(direct(t * n_sub + s, t, s).start)

    def list_up(rank, t, s):
        @pl.when(above(rank, t, s) & (s != sub))
        def _():
            pl.semaphore_wait(here_sems.at[rank], 1)
            direct(rank, t, s).start()
            for back in range(n_tm):
                pl.when((t == tm) & (back < tm))(direct(back * n_sub + s, back, s).start)

    each_owner(list_up)

    def landed(rank):
        held = lists_ref.at[rank]
        return send(held, held, list_send.at[0], list_recv.at[rank], {"ch": other})

    own_tile = me * (span // n_sub // LANES)
    early = (sub != n_sub - 1) | (tm == 0) | (tm == n_tm - 1)

    def prepare():
        own_columns(series_ref, own_tile, mine_ref, norms_ref)

    for step in range(1, n_tm):
        source = step + ((tm + n_tm - step) // n_tm) * (tm - 2 * step)
        held = chunk(source, ch)
        send(held, held, time_send.at[0], time_recv.at[source], {"ch": other}).wait_recv()
        forward(held)
        if step == 1:
            for copy in to_pair:
                copy.wait_recv()
            pl.when(early)(prepare)
    each_owner(lambda rank, t, s: pl.when(rank != me)(landed(rank).wait_recv))
    keep = pltpu.make_async_copy(lists_ref, lists_smem, load_sems.at[0])
    keep.start()
    swap.wait_send()
    for t in range(n_tm):
        pl.when(t != tm)(along_time(t).wait_send)
    each_owner(lambda rank, t, s: pl.when(rank != me)(direct(rank, t, s).wait_send))
    for copy in to_pair:
        copy.wait_send()
    for copy in to_pair[2:]:
        copy.wait_recv()
    pl.when(jnp.logical_not(early))(prepare)
    keep.wait()


def match_kernel(
    n_sub,
    series_ref,
    lists_smem,
    mine_ref,
    norms_ref,
    out_ref,
    work_smem,
    lagged_ref,
    wide_ref,
    products_ref,
    best_ref,
):
    units, unit_cols, _ = mine_ref.shape
    n_tiles = unit_cols // LANES
    unit = unit_cols - M
    per_block = TS // LANES
    rows = TS + M
    tm, ch = lax.axis_index("tm"), lax.axis_index("ch")
    me = tm * n_sub + lax.axis_index("sub")
    share = jnp.where(tm == 0, 1 - ch, ch)
    own_tile = me * (units * unit // LANES)
    for u in range(units):
        for s in range(PAIRED):
            best_ref[s, u] = jnp.full((8, unit_cols), jnp.inf, jnp.float32)
    lane = lax.broadcasted_iota(jnp.int32, (8, LANES), 1)
    own_at = [((lane // STEP) * n_tiles + t) * STEP + lane % STEP for t in range(n_tiles)]
    sublane = lax.broadcasted_iota(jnp.int32, (8, LANES), 0)

    owners = lists_smem.shape[0]

    def scan(owner, found):
        for slot in range(SLOTS):
            row_block, col_block = lists_smem[owner, slot, 0], lists_smem[owner, slot, 1]
            for u in range(units):
                block = (own_tile * LANES + u * unit) // TS
                work_smem[found] = (row_block + col_block - block) * units + u
                hit = (row_block == block) | (col_block == block)
                found = found + hit.astype(jnp.int32)
        return found

    if owners <= 16:
        found = jnp.int32(0)
        for owner in range(owners):
            found = scan(owner, found)
    else:
        found = lax.fori_loop(0, owners, scan, jnp.int32(0))

    def ahead(tiles, at):
        turn = at // n_tiles
        tile = tiles[at % n_tiles]
        return tile if turn == 0 else pltpu.roll(tile, LANES - turn * STEP, axis=1)

    def keep_apart(s, offset):
        for g in range(lines // STEP):
            if g % (M // STEP) < JOIN:
                for at in range(g * STEP, (g + 1) * STEP, 8):
                    for t in range(n_tiles):
                        here = (s, pl.ds(at, 8), pl.ds(t * LANES, LANES))
                        apart = (sublane + (at + offset)) - own_at[t]
                        products_ref[here] = jnp.where(
                            jnp.abs(apart) < EXCL, jnp.inf, products_ref[here]
                        )

    def reduce(s, u):
        low = [best_ref[s, u, :, t * LANES : (t + 1) * LANES] for t in range(n_tiles)]
        for part in range(0, STEP, 8):
            sums = {}
            for g in range(lines // STEP):
                at = g * STEP + part
                sums[JOIN, g] = [
                    products_ref[s, at : at + 8, t * LANES : (t + 1) * LANES] for t in range(n_tiles)
                ]
                first, size = g, JOIN
                while size < M // STEP and first >= size:
                    first -= size
                    early, late = sums[size, first], sums[size, first + size]
                    sums[2 * size, first] = [
                        early[t] + ahead(late, t + size) for t in range(n_tiles)
                    ]
                    size *= 2
                if size == M // STEP:
                    at = first * STEP + part
                    wide = wide_ref[s, at : at + 8, :]
                    for t in range(n_tiles):
                        low[t] = jnp.minimum(low[t], sums[size, first][t] + wide)
        for t in range(n_tiles):
            best_ref[s, u, :, t * LANES : (t + 1) * LANES] = low[t]

    lines = products_ref.shape[1]

    def shift(s, entry):
        lagged, norms = lag(series_ref, (entry // units) * per_block, rows // LANES, -2.0)
        place = 0
        for piece in lagged:
            lagged_ref[s, place : place + piece.shape[0], :] = piece
            place += piece.shape[0]
        for k in range(per_block):
            one = jnp.broadcast_to(norms[:1, k * LANES : (k + 1) * LANES], (LANES, LANES))
            wide_ref[s, k * LANES : (k + 1) * LANES, :] = jnp.transpose(one)

    def multiply(s, entry):
        longer = [lagged_ref[s, v * STEP : v * STEP + lines, :] for v in range(JOIN)]
        products_ref[s] = lax.dot_general(
            jnp.concatenate(longer, axis=1) if JOIN > 1 else longer[0],
            mine_ref[entry % units],
            (((1,), (1,)), ((), ())),
            preferred_element_type=jnp.float32,
        )

    def lower(s, entry):
        u = entry % units
        keep_apart(s, (entry // units) * TS - (own_tile * LANES + u * unit))
        reduce(s, u)

    share_count = (found + 1 - share) // 2

    def couple(at, _):
        entries = [
            work_smem[2 * (at * PAIRED + s) + share] for s in range(PAIRED)
        ]
        shift(0, entries[0])
        multiply(0, entries[0])
        shift(1, entries[1])
        multiply(1, entries[1])
        lower(0, entries[0])
        lower(1, entries[1])
        return 0

    lax.fori_loop(0, share_count // PAIRED, couple, 0)

    @pl.when(share_count % PAIRED == 1)
    def _():
        entry = work_smem[2 * (share_count - 1) + share]
        shift(0, entry)
        multiply(0, entry)
        lower(0, entry)

    group = lane // STEP
    for u in range(units):
        low = jnp.min(jnp.min(best_ref[:, u], axis=0), axis=0, keepdims=True)
        tiles = [
            jnp.broadcast_to(low[:, t * LANES : (t + 1) * LANES], (8, LANES)) for t in range(n_tiles)
        ]
        for k in range(unit // LANES):
            natural = None
            for g in range(LANES // STEP):
                q = k * (LANES // STEP) + g
                turn = (g - q // n_tiles) % (LANES // STEP)
                tile = tiles[q % n_tiles]
                tile = tile if turn == 0 else pltpu.roll(tile, turn * STEP, axis=1)
                natural = tile if natural is None else jnp.where(group == g, tile, natural)
            at = u * (unit // LANES) + k
            done = (natural[:1] + norms_ref[:1, at * LANES : (at + 1) * LANES]) * (1.0 / DEPTH)
            out_ref[at : at + 1, :] = done


def swap_kernel(mine_ref, theirs_ref, sems):
    other = {"ch": 1 - lax.axis_index("ch")}
    barrier = pltpu.get_barrier_semaphore()
    pl.semaphore_signal(barrier, inc=1, device_id=other, device_id_type=MESH)
    pl.semaphore_wait(barrier, 1)
    copy = pltpu.make_async_remote_copy(
        src_ref=mine_ref,
        dst_ref=theirs_ref,
        send_sem=sems.at[0],
        recv_sem=sems.at[1],
        device_id=other,
        device_id_type=MESH,
    )
    copy.start()
    copy.wait()


def lower_kernel(mine_ref, theirs_ref, out_ref):
    out_ref[...] = jnp.minimum(mine_ref[...], theirs_ref[...])


def body(archive, tail, precision, tile_list):
    n_tm, n_sub = lax.axis_size("tm"), lax.axis_size("sub")
    owners = n_tm * n_sub
    channels, span = archive.shape
    piece = span // n_sub
    unit = min(piece, TS)
    units = piece // unit
    every = 2 * channels
    depth = STEP * every
    anywhere = pl.BlockSpec(memory_space=pltpu.HBM)
    inside = pl.BlockSpec(memory_space=pltpu.VMEM)
    scalars = pl.BlockSpec(memory_space=pltpu.SMEM)
    series, lists, own, norms = pl.pallas_call(
        functools.partial(gather_kernel, n_tm, n_sub),
        out_shape=[
            pltpu.VMEM((n_tm * span // LANES + 1, every, LANES), jnp.bfloat16),
            pltpu.SMEM((owners,) + tile_list.shape[2:], jnp.int32),
            pltpu.VMEM((units, unit + M, JOIN * depth), jnp.bfloat16),
            pltpu.VMEM((8, piece + M), jnp.float32),
        ],
        in_specs=[anywhere] * 4,
        out_specs=[inside, scalars, inside, inside],
        scratch_shapes=[
            pltpu.VMEM((owners,) + tile_list.shape[2:], jnp.int32),
            pltpu.VMEM(tail.shape, jnp.float32),
            pltpu.VMEM(precision.shape, jnp.float32),
            pltpu.VMEM((every, span // 2), jnp.float32),
            pltpu.SemaphoreType.DMA((4,)),
            pltpu.SemaphoreType.DMA((2,)),
            pltpu.SemaphoreType.DMA((n_tm,)),
            pltpu.SemaphoreType.DMA((n_tm,)),
            pltpu.SemaphoreType.DMA((n_tm,)),
            pltpu.SemaphoreType.DMA((n_tm,)),
            pltpu.SemaphoreType.DMA((owners,)),
            pltpu.SemaphoreType.DMA((owners,)),
            pltpu.SemaphoreType.REGULAR((owners,)),
        ],
        compiler_params=pltpu.CompilerParams(
            collective_id=0, has_side_effects=True, vmem_limit_bytes=62 * 2**20
        ),
    )(tile_list, archive, tail, precision)
    series, own, norms = [
        pltpu.with_memory_space_constraint(array, pltpu.VMEM) for array in (series, own, norms)
    ]
    lists = pltpu.with_memory_space_constraint(lists, pltpu.SMEM)
    shape = (piece // LANES, LANES)
    mine = pl.pallas_call(
        functools.partial(match_kernel, n_sub),
        out_shape=pltpu.VMEM(shape, jnp.float32),
        in_specs=[inside, scalars, inside, inside],
        out_specs=inside,
        scratch_shapes=[
            pltpu.SMEM((owners * SLOTS * units + 1,), jnp.int32),
            pltpu.VMEM((PAIRED, TS + M, depth), jnp.bfloat16),
            pltpu.VMEM((PAIRED, TS, LANES), jnp.float32),
            pltpu.VMEM((PAIRED, TS + M - JOIN * STEP, unit + M), jnp.float32),
            pltpu.VMEM((PAIRED, units, 8, unit + M), jnp.float32),
        ],
        compiler_params=pltpu.CompilerParams(vmem_limit_bytes=32 * 2**20),
    )(series, lists, own, norms)
    mine = pltpu.with_memory_space_constraint(mine, pltpu.VMEM)
    theirs = pl.pallas_call(
        swap_kernel,
        out_shape=pltpu.VMEM(shape, jnp.float32),
        in_specs=[inside],
        out_specs=inside,
        scratch_shapes=[pltpu.SemaphoreType.DMA((2,))],
        compiler_params=pltpu.CompilerParams(
            collective_id=1, has_side_effects=True, vmem_limit_bytes=16 * 2**20
        ),
    )(mine)
    theirs = pltpu.with_memory_space_constraint(theirs, pltpu.VMEM)
    out = pl.pallas_call(
        lower_kernel,
        out_shape=jax.ShapeDtypeStruct(shape, jnp.float32),
        in_specs=[inside] * 2,
        out_specs=inside,
        compiler_params=pltpu.CompilerParams(vmem_limit_bytes=16 * 2**20),
    )(mine, theirs)
    return out.reshape(-1)


def solution(mesh):
    placed = (P("ch", ("grp", "tm")), P(None, "grp"), P(), P(("grp", "tm"), "sub", None, None))
    return jax.shard_map(
        body, mesh=mesh, in_specs=placed, out_specs=P(("grp", "tm", "sub")), check_vma=False
    )
```

profile of v0, /device:TPU:0, one launch (start us, length us, event | category | flops | bytes accessed | tf_op | source)
XLA Modules:
  0.0 15.3 jit_solution(7382612385298179884)
XLA Ops:
  0.0 10.3 %shard_map.46 = (bf16[65,16,128]{2,1,0:T(8,128)(2,1)S(1)}, s32[8,2,2]{2,1,0:T(2,128)S(4)}, bf16[2,640,512]{2,1,0:T(8,128)(2,1)S(1)}, f32[8,1152]{1,0:T(8,128)S(1)}) custom-call(s32[1,1,2,2]{3,2,1,0:T(2,128)} %tiles_hbm.1, f32[8,2048]{1,0:T(8,128)} %archive_hbm.1, f32[16,127]{1,0:T(8,128)} %tail_hbm.1, f32[16,16]{1,0:T(8,128)} %precision_hbm.1), custom_call_target="tpu_custom_call" | custom-call | tf_op jit(solution)/shard_map/pallas_call | solution.py:484
  10.3 3.1 %shard_map.47.mine_ref = f32[8,128]{1,0:T(8,128)S(1)} custom-call(bf16[65,16,128]{2,1,0:T(8,128)(2,1)S(1)} %get-tuple-element.9.series_ref, s32[8,2,2]{2,1,0:T(2,128)S(4)} %get-tuple-element.10.lists_smem, bf16[2,640,512]{2,1,0:T(8,128)(2,1)S(1)} %get-tuple-element.11.mine_ref, f32[8,1152]{1,0:T(8,128)S(1)} %get-tuple-element.12.norms_ref), custom_call_target="tpu_custom_call" | custom-call | tf_op jit(solution)/shard_map/pallas_call | solution.py:518
  13.4 1.2 %shard_map.48.theirs_ref = f32[8,128]{1,0:T(8,128)S(1)} custom-call(f32[8,128]{1,0:T(8,128)S(1)} %shard_map.47.mine_ref), custom_call_target="tpu_custom_call" | custom-call | tf_op jit(solution)/shard_map/pallas_call | solution.py:533
  14.7 0.6 %shard_map.49 = f32[8,128]{1,0:T(8,128)} custom-call(f32[8,128]{1,0:T(8,128)S(1)} %shard_map.47.mine_ref, f32[8,128]{1,0:T(8,128)S(1)} %shard_map.48.theirs_ref), custom_call_target="tpu_custom_call" | custom-call | tf_op jit(solution)/shard_map/pallas_call | solution.py:544
where the time goes:
time: 15.5 us; the launch traced here: 15.3 us
  Pallas kernels  15.2 us (98%)
    pallas_call x1, Pallas kernels, body(): pl.pallas_call(functools.partial(gather_kernel, n_tm, n_sub), out_shape=[...  10.3 us
    pallas_call x1, Pallas kernels, body(): pl.pallas_call(functools.partial(match_kernel, n_sub), out_shape=pltpu.VM...  3.13 us
    pallas_call x1, Pallas kernels, body(): pl.pallas_call(swap_kernel, out_shape=pltpu.VMEM(shape, jnp.float32), in_...  1.23 us
    pallas_call x1, Pallas kernels, body(): pl.pallas_call(lower_kernel, out_shape=jax.ShapeDtypeStruct(shape, jnp.fl...  0.6 us

commit v1 on v0

--- a/solution.py
+++ b/solution.py
@@ -15,7 +15,7 @@
 LANES = 128
 STEP = 16
 JOIN = 2
-PAIRED = 2
+PAIRED = 3
 MESH = pl.DeviceIdType.MESH
 
 
@@ -408,26 +408,33 @@
 
     share_count = (found + 1 - share) // 2
 
+    def together(first, count):
+        entries = [work_smem[2 * (first + s) + share] for s in range(count)]
+        for s in range(count):
+            shift(s, entries[s])
+            multiply(s, entries[s])
+        for s in range(count):
+            lower(s, entries[s])
+
+    triples = jnp.where(
+        share_count % 3 == 1, jnp.maximum(share_count // 3 - 1, 0), share_count // 3
+    )
+    rest = share_count - 3 * triples
+
+    def triple(at, _):
+        together(3 * at, 3)
+        return 0
+
     def couple(at, _):
-        entries = [
-            work_smem[2 * (at * PAIRED + s) + share] for s in range(PAIRED)
-        ]
-        shift(0, entries[0])
-        multiply(0, entries[0])
-        shift(1, entries[1])
-        multiply(1, entries[1])
-        lower(0, entries[0])
-        lower(1, entries[1])
+        together(3 * triples + 2 * at, 2)
         return 0
 
-    lax.fori_loop(0, share_count // PAIRED, couple, 0)
-
-    @pl.when(share_count % PAIRED == 1)
+    lax.fori_loop(0, triples, triple, 0)
+    lax.fori_loop(0, rest // 2, couple, 0)
+
+    @pl.when(rest % 2 == 1)
     def _():
-        entry = work_smem[2 * (share_count - 1) + share]
-        shift(0, entry)
-        multiply(0, entry)
-        lower(0, entry)
+        together(share_count - 1, 1)
 
     group = lane // STEP
     for u in range(units):

time: 15.5 us -> 15.1 us (0.974)
  Pallas kernels: 15.2 us -> 14.9 us
    pallas_call x1, Pallas kernels: 3.13 us -> 2.07 us  [body(): pl.pallas_call(functools.partial(match_kernel, n_sub), out_shape=pltpu.VM...]
    pallas_call x1, Pallas kernels: 1.23 us -> 1.96 us  [body(): pl.pallas_call(swap_kernel, out_shape=pltpu.VMEM(shape, jnp.float32), in_...]
where the time goes in v1:
time: 15.1 us; the launch traced here: 14.9 us
  Pallas kernels  14.9 us (99%)
    pallas_call x1, Pallas kernels, body(): pl.pallas_call(functools.partial(gather_kernel, n_tm, n_sub), out_shape=[...  10.3 us
    pallas_call x1, Pallas kernels, body(): pl.pallas_call(functools.partial(match_kernel, n_sub), out_shape=pltpu.VM...  2.07 us
    pallas_call x1, Pallas kernels, body(): pl.pallas_call(swap_kernel, out_shape=pltpu.VMEM(shape, jnp.float32), in_...  1.96 us
    pallas_call x1, Pallas kernels, body(): pl.pallas_call(lower_kernel, out_shape=jax.ShapeDtypeStruct(shape, jnp.fl...  0.6 us

profile of v1, /device:TPU:0, one launch (start us, length us, event | category | flops | bytes accessed | tf_op | source)
XLA Modules:
  0.0 14.9 jit_solution(14501377949766940644)
XLA Ops:
  0.0 10.3 %shard_map.46 = (bf16[65,16,128]{2,1,0:T(8,128)(2,1)S(1)}, s32[8,2,2]{2,1,0:T(2,128)S(4)}, bf16[2,640,512]{2,1,0:T(8,128)(2,1)S(1)}, f32[8,1152]{1,0:T(8,128)S(1)}) custom-call(s32[1,1,2,2]{3,2,1,0:T(2,128)} %tiles_hbm.1, f32[8,2048]{1,0:T(8,128)} %archive_hbm.1, f32[16,127]{1,0:T(8,128)} %tail_hbm.1, f32[16,16]{1,0:T(8,128)} %precision_hbm.1), custom_call_target="tpu_custom_call" | custom-call | tf_op jit(solution)/shard_map/pallas_call | solution.py:491
  10.3 2.1 %shard_map.47.mine_ref = f32[8,128]{1,0:T(8,128)S(1)} custom-call(bf16[65,16,128]{2,1,0:T(8,128)(2,1)S(1)} %get-tuple-element.9.series_ref, s32[8,2,2]{2,1,0:T(2,128)S(4)} %get-tuple-element.10.lists_smem, bf16[2,640,512]{2,1,0:T(8,128)(2,1)S(1)} %get-tuple-element.11.mine_ref, f32[8,1152]{1,0:T(8,128)S(1)} %get-tuple-element.12.norms_ref), custom_call_target="tpu_custom_call" | custom-call | tf_op jit(solution)/shard_map/pallas_call | solution.py:525
  12.4 2.0 %shard_map.48.theirs_ref = f32[8,128]{1,0:T(8,128)S(1)} custom-call(f32[8,128]{1,0:T(8,128)S(1)} %shard_map.47.mine_ref), custom_call_target="tpu_custom_call" | custom-call | tf_op jit(solution)/shard_map/pallas_call | solution.py:540
  14.3 0.6 %shard_map.49 = f32[8,128]{1,0:T(8,128)} custom-call(f32[8,128]{1,0:T(8,128)S(1)} %shard_map.47.mine_ref, f32[8,128]{1,0:T(8,128)S(1)} %shard_map.48.theirs_ref), custom_call_target="tpu_custom_call" | custom-call | tf_op jit(solution)/shard_map/pallas_call | solution.py:551

commit v2 on v1

--- a/solution.py
+++ b/solution.py
@@ -15,7 +15,7 @@
 LANES = 128
 STEP = 16
 JOIN = 2
-PAIRED = 3
+PAIRED = 4
 MESH = pl.DeviceIdType.MESH
 
 
@@ -416,25 +416,14 @@
         for s in range(count):
             lower(s, entries[s])
 
-    triples = jnp.where(
-        share_count % 3 == 1, jnp.maximum(share_count // 3 - 1, 0), share_count // 3
-    )
-    rest = share_count - 3 * triples
-
-    def triple(at, _):
-        together(3 * at, 3)
+    def four(at, _):
+        together(4 * at, 4)
         return 0
 
-    def couple(at, _):
-        together(3 * triples + 2 * at, 2)
-        return 0
-
-    lax.fori_loop(0, triples, triple, 0)
-    lax.fori_loop(0, rest // 2, couple, 0)
-
-    @pl.when(rest % 2 == 1)
-    def _():
-        together(share_count - 1, 1)
+    fours = share_count // 4
+    lax.fori_loop(0, fours, four, 0)
+    for count in (3, 2, 1):
+        pl.when(share_count % 4 == count)(functools.partial(together, 4 * fours, count))
 
     group = lane // STEP
     for u in range(units):

time: 15.1 us -> 15.1 us (level)
  no operation moved by 1% of the time
where the time goes in v2:
time: 15.1 us; the launch traced here: 14.9 us
  Pallas kernels  14.9 us (99%)
    pallas_call x1, Pallas kernels, body(): pl.pallas_call(functools.partial(gather_kernel, n_tm, n_sub), out_shape=[...  10.3 us
    pallas_call x1, Pallas kernels, body(): pl.pallas_call(functools.partial(match_kernel, n_sub), out_shape=pltpu.VM...  2.06 us
    pallas_call x1, Pallas kernels, body(): pl.pallas_call(swap_kernel, out_shape=pltpu.VMEM(shape, jnp.float32), in_...  1.96 us
    pallas_call x1, Pallas kernels, body(): pl.pallas_call(lower_kernel, out_shape=jax.ShapeDtypeStruct(shape, jnp.fl...  0.6 us

profile of v2, /device:TPU:0, one launch (start us, length us, event | category | flops | bytes accessed | tf_op | source)
XLA Modules:
  0.0 14.9 jit_solution(8584992468301006160)
XLA Ops:
  0.0 10.3 %shard_map.46 = (bf16[65,16,128]{2,1,0:T(8,128)(2,1)S(1)}, s32[8,2,2]{2,1,0:T(2,128)S(4)}, bf16[2,640,512]{2,1,0:T(8,128)(2,1)S(1)}, f32[8,1152]{1,0:T(8,128)S(1)}) custom-call(s32[1,1,2,2]{3,2,1,0:T(2,128)} %tiles_hbm.1, f32[8,2048]{1,0:T(8,128)} %archive_hbm.1, f32[16,127]{1,0:T(8,128)} %tail_hbm.1, f32[16,16]{1,0:T(8,128)} %precision_hbm.1), custom_call_target="tpu_custom_call" | custom-call | tf_op jit(solution)/shard_map/pallas_call | solution.py:480
  10.3 2.1 %shard_map.47.mine_ref = f32[8,128]{1,0:T(8,128)S(1)} custom-call(bf16[65,16,128]{2,1,0:T(8,128)(2,1)S(1)} %get-tuple-element.9.series_ref, s32[8,2,2]{2,1,0:T(2,128)S(4)} %get-tuple-element.10.lists_smem, bf16[2,640,512]{2,1,0:T(8,128)(2,1)S(1)} %get-tuple-element.11.mine_ref, f32[8,1152]{1,0:T(8,128)S(1)} %get-tuple-element.12.norms_ref), custom_call_target="tpu_custom_call" | custom-call | tf_op jit(solution)/shard_map/pallas_call | solution.py:514
  12.4 2.0 %shard_map.48.theirs_ref = f32[8,128]{1,0:T(8,128)S(1)} custom-call(f32[8,128]{1,0:T(8,128)S(1)} %shard_map.47.mine_ref), custom_call_target="tpu_custom_call" | custom-call | tf_op jit(solution)/shard_map/pallas_call | solution.py:529
  14.3 0.6 %shard_map.49 = f32[8,128]{1,0:T(8,128)} custom-call(f32[8,128]{1,0:T(8,128)S(1)} %shard_map.47.mine_ref, f32[8,128]{1,0:T(8,128)S(1)} %shard_map.48.theirs_ref), custom_call_target="tpu_custom_call" | custom-call | tf_op jit(solution)/shard_map/pallas_call | solution.py:540
